TPU v7x, 256 devices: a whole 4x4x8 slice. The times are simulated.
256 devices in a mesh: pipe: 64 (over x, y, z_hi, core), dp: 4 (over z_lo).
Axes of the slice: x: 4, y: 4, z: 8 (z_hi: 2, z_lo: 4; z = z_hi * 4 + z_lo), core: 2. Of those that a mesh axis runs over, the one named last changes fastest.
Arguments:
- lead_front: bfloat16 [64, 512, 3072], P('pipe', 'dp'), may hold values from -19 to 19
- mirror_front: bfloat16 [64, 512, 3072], P('pipe', 'dp'), may hold values from -19 to 19
- lead_grad: bfloat16 [64, 512, 3072], P('pipe', 'dp'), may hold values from -19 to 19
- mirror_grad: bfloat16 [64, 512, 3072], P('pipe', 'dp'), may hold values from -19 to 19
- lead_saved: bfloat16 [64, 2, 512, 3072], P('pipe', None, 'dp'), may hold values from -19 to 19
- mirror_saved: bfloat16 [64, 2, 512, 3072], P('pipe', None, 'dp'), may hold values from -19 to 19
- lead_down: bfloat16 [64, 3072, 256], P('pipe', 'dp'), may hold values from -0.109375 to 0.109375
- lead_up: bfloat16 [64, 256, 3072], P('pipe', None, 'dp'), may hold values from -0.375 to 0.375
- mirror_down: bfloat16 [64, 3072, 256], P('pipe', 'dp'), may hold values from -0.109375 to 0.109375
- mirror_up: bfloat16 [64, 256, 3072], P('pipe', None, 'dp'), may hold values from -0.375 to 0.375
Outputs:
- lead_out: bfloat16 [64, 512, 3072], P('pipe', 'dp')
- mirror_out: bfloat16 [64, 512, 3072], P('pipe', 'dp')
- lead_dx: bfloat16 [64, 512, 3072], P('pipe', 'dp')
- mirror_dx: bfloat16 [64, 512, 3072], P('pipe', 'dp')
- lead_down_grad: bfloat16 [64, 3072, 256], P('pipe', 'dp')
- lead_up_grad: bfloat16 [64, 256, 3072], P('pipe', None, 'dp')
- mirror_down_grad: bfloat16 [64, 3072, 256], P('pipe', 'dp')
- mirror_up_grad: bfloat16 [64, 256, 3072], P('pipe', None, 'dp')
All inputs are finite; a program needn't handle non-finite values.
Results may differ from a plain program's by a relative error of at most 0.013.
Values may be sent and summed in bfloat16 or wider, within the bound.
A program may use at most 128 MiB of HBM per device.

v0:
```python
import jax
import jax.numpy as jnp
from jax import lax
from jax.sharding import PartitionSpec as P

EPS = 1e-06


def passed_along(value, axis, steps):
    count = lax.axis_size(axis)
    initial, last = (max(0, -steps), min(count, count - steps))
    return lax.ppermute(value, axis, [(source, source + steps) for source in range(initial, last)])


def normalize(inputs):
    float_in = inputs.astype(jnp.float32)
    factor = lax.rsqrt(jnp.mean(float_in * float_in, axis=-1, keepdims=True) + EPS)
    return (float_in, factor)


def section_forward(inputs, w_down, w_up):
    float_in, factor = normalize(inputs)
    normed = (float_in * factor).astype(jnp.bfloat16)
    latent = jnp.dot(normed, w_down, preferred_element_type=jnp.float32)
    active = jax.nn.silu(latent).astype(jnp.bfloat16)
    return (float_in + jnp.dot(active, w_up, preferred_element_type=jnp.float32)).astype(
        jnp.bfloat16
    )


def section_backward(stored, incoming, w_down, w_up):
    float_in, factor = normalize(stored)
    scaled = float_in * factor
    normed = scaled.astype(jnp.bfloat16)
    latent = jnp.dot(normed, w_down, preferred_element_type=jnp.float32)
    active = jax.nn.silu(latent).astype(jnp.bfloat16)
    d_active = lax.dot_general(
        incoming, w_up, (((1,), (1,)), ((), ())), preferred_element_type=jnp.float32
    )
    squash = jax.nn.sigmoid(latent)
    d_latent = (d_active * squash * (1.0 + latent * (1.0 - squash))).astype(jnp.bfloat16)
    d_normed = lax.dot_general(
        d_latent, w_down, (((1,), (1,)), ((), ())), preferred_element_type=jnp.float32
    )
    inner_mean = jnp.mean(d_normed * scaled, axis=-1, keepdims=True)
    d_inputs = (incoming.astype(jnp.float32) + factor * (d_normed - scaled * inner_mean)).astype(
        jnp.bfloat16
    )
    return (d_inputs, normed, d_latent, active)


def contract_rows(left_rows, right_rows):
    return lax.dot_general(
        left_rows, right_rows, (((0,), (0,)), ((), ())), preferred_element_type=jnp.float32
    )


def send_upward(stacked):
    return passed_along(stacked, "pipe", 1)


def send_downward(stacked):
    return passed_along(stacked, "pipe", -1)


def body(
    lead_front,
    mirror_front,
    lead_grad,
    mirror_grad,
    lead_saved,
    mirror_saved,
    lead_down,
    lead_up,
    mirror_down,
    mirror_up,
):
    whole_weights = (
        lax.all_gather(lead_down, "dp", axis=1, tiled=True),
        lax.all_gather(lead_up, "dp", axis=2, tiled=True),
        lax.all_gather(mirror_down, "dp", axis=1, tiled=True),
        lax.all_gather(mirror_up, "dp", axis=2, tiled=True),
    )
    weight_pairs = (
        (whole_weights[0][0], whole_weights[1][0]),
        (whole_weights[2][0], whole_weights[3][0]),
    )
    stored = (lead_saved[0], mirror_saved[0])
    fronts = (lead_front[0], mirror_front[0])
    arriving = (lead_grad[0], mirror_grad[0])
    tick_count = lead_saved.shape[1]
    row_count = lead_front.shape[1]
    pieces = 1
    stretch = row_count // pieces
    operands = [[[], [], [], []], [[], [], [], []]]
    for moment in range(tick_count):
        next_fronts = [[], []]
        next_arriving = [[], []]
        produced = []
        returned = []
        for member in range(2):
            w_down, w_up = weight_pairs[member]
            produced.append(section_forward(fronts[member], w_down, w_up))
            incoming = arriving[member]
            d_inputs, normed, d_latent, active = section_backward(
                stored[member][moment, 0:stretch], incoming, w_down, w_up
            )
            returned.append(d_inputs)
            operands[member][0].append(normed)
            operands[member][1].append(incoming)
            operands[member][2].append(d_latent)
            operands[member][3].append(active)
        if moment + 1 < tick_count:
            upward = send_upward(jnp.stack([produced[0], returned[1]]))
            behind = send_downward(jnp.stack([produced[1], returned[0]]))
            next_fronts[0].append(upward[0])
            next_arriving[1].append(upward[1])
            next_fronts[1].append(behind[0])
            next_arriving[0].append(behind[1])
        else:
            next_fronts[0].append(produced[0])
            next_fronts[1].append(produced[1])
            next_arriving[0].append(returned[0])
            next_arriving[1].append(returned[1])
        fronts = (jnp.concatenate(next_fronts[0], 0), jnp.concatenate(next_fronts[1], 0))
        arriving = (jnp.concatenate(next_arriving[0], 0), jnp.concatenate(next_arriving[1], 0))
    joined = [
        [jnp.concatenate(collected, 0) for collected in operands[member]] for member in range(2)
    ]
    columns = (
        lax.all_to_all(joined[0][0], "dp", split_axis=1, concat_axis=0, tiled=True),
        lax.all_to_all(joined[0][1], "dp", split_axis=1, concat_axis=0, tiled=True),
        lax.all_to_all(joined[1][0], "dp", split_axis=1, concat_axis=0, tiled=True),
        lax.all_to_all(joined[1][1], "dp", split_axis=1, concat_axis=0, tiled=True),
    )
    latents = (
        lax.all_gather(joined[0][2], "dp", axis=0, tiled=True),
        lax.all_gather(joined[0][3], "dp", axis=0, tiled=True),
        lax.all_gather(joined[1][2], "dp", axis=0, tiled=True),
        lax.all_gather(joined[1][3], "dp", axis=0, tiled=True),
    )
    gradients = (
        contract_rows(columns[0], latents[0]),
        contract_rows(latents[1], columns[1]),
        contract_rows(columns[2], latents[2]),
        contract_rows(latents[3], columns[3]),
    )
    return (
        fronts[0][None],
        fronts[1][None],
        arriving[0][None],
        arriving[1][None],
        gradients[0].astype(jnp.bfloat16)[None],
        gradients[1].astype(jnp.bfloat16)[None],
        gradients[2].astype(jnp.bfloat16)[None],
        gradients[3].astype(jnp.bfloat16)[None],
    )


def solution(mesh):
    placed = (
        P("pipe", "dp", None),
        P("pipe", "dp", None),
        P("pipe", "dp", None),
        P("pipe", "dp", None),
        P("pipe", None, "dp", None),
        P("pipe", None, "dp", None),
        P("pipe", "dp", None),
        P("pipe", None, "dp"),
        P("pipe", "dp", None),
        P("pipe", None, "dp"),
    )
    return jax.shard_map(
        body,
        mesh=mesh,
        in_specs=placed,
        out_specs=(
            P("pipe", "dp", None),
            P("pipe", "dp", None),
            P("pipe", "dp", None),
            P("pipe", "dp", None),
            P("pipe", "dp", None),
            P("pipe", None, "dp"),
            P("pipe", "dp", None),
            P("pipe", None, "dp"),
        ),
        check_vma=False,
    )
```

profile of v0, /device:TPU:6, one launch (start us, length us, event | category | flops | bytes accessed | tf_op | source)
XLA Modules:
  0.0 507.6 jit_solution(11541942165054088550)
XLA Ops:
  7.2 0.7 all-gather.5.cloned.1.call-update
  8.0 0.7 all-gather.7.cloned.1.call-update
  8.7 0.7 all-gather.9.cloned.1.call-update
  10.0 1.4 fusion.22
  11.4 2.0 slice_convert_fusion.2
  13.6 2.0 slice_convert_fusion.3
  16.2 2.9 reshape.249
  19.1 2.9 reshape.248
  22.0 2.9 reshape.251
  25.0 3.0 reshape.250
  27.9 2.8 fusion.63
  30.7 1.3 fusion.61
  32.0 22.5 %all-gather.5.cloned.1.call-done = bf16[1,3072,256]{2,1,0:T(8,128)(2,1)} async-done(((bf16[1,768,256]{2,1,0:T(8,128)(2,1)}), bf16[1,3072,256]{2,1,0:T(8,128)(2,1)}) %all-gather.5.cloned.1.call-update) | async-done | bytes 1572880 | tf_op jit(solution)/shard_map/all_gather | solution.py:79
  54.5 1.8 multiply_convert_fusion.7
  56.3 41.1 %all-gather.7.cloned.1.call-done = bf16[1,256,3072]{2,1,0:T(8,128)(2,1)} async-done(((bf16[1,256,768]{2,1,0:T(8,128)(2,1)}), bf16[1,256,3072]{2,1,0:T(8,128)(2,1)}) %all-gather.7.cloned.1.call-update) | async-done | bytes 1572880 | tf_op jit(solution)/shard_map/all_gather | solution.py:80
  97.4 2.4 fusion.101
  99.9 2.0 fusion.21
  102.3 0.7 copy-done.14
  103.0 1.3 pad_maximum_fusion.2
  104.2 4.4 all-to-all-start
  108.6 3.0 fusion.109
  111.7 51.1 %all-gather.9.cloned.1.call-done = bf16[1,256,3072]{2,1,0:T(8,128)(2,1)} async-done(((bf16[1,256,768]{2,1,0:T(8,128)(2,1)}), bf16[1,256,3072]{2,1,0:T(8,128)(2,1)}) %all-gather.9.cloned.1.call-update) | async-done | bytes 1572880 | tf_op jit(solution)/shard_map/all_gather | solution.py:82
  162.7 49.0 %all-gather.11.cloned.1.call-done = bf16[1,3072,256]{2,1,0:T(8,128)(2,1)} async-done(((bf16[1,768,256]{2,1,0:T(8,128)(2,1)}), bf16[1,3072,256]{2,1,0:T(8,128)(2,1)}) %all-gather.11.cloned.1.call-update) | async-done | bytes 1572880 | tf_op jit(solution)/shard_map/all_gather | solution.py:81
  211.7 4.3 fusion.5
  216.0 2.8 pad_maximum_fusion.1
  218.8 8.2 %collective-permute-start.1 = (bf16[2,128,3072]{2,1,0:T(8,128)(2,1)}, bf16[2,128,3072]{2,1,0:T(8,128)(2,1)}, u32[]{:S(2)}, u32[]{:S(2)}) collective-permute-start(bf16[2,128,3072]{2,1,0:T(8,128)(2,1)} %pad_maximum_fusion.1), channel_id=1, source_target_pairs={{4,0},{8,4},{12,8},{16,12},{20,16},{24,20},{28,24},{32,28},{36,32}... | collective-permute-start | bytes 4718600 | tf_op jit(solution)/shard_map/ppermute | solution.py:12
  228.2 1.9 fusion.20
  230.5 0.7 copy-done.13
  231.2 1.3 pad_maximum_fusion.4
  232.5 4.3 fusion.7
  236.8 4.4 all-to-all-start.2
  241.1 2.2 fusion.106
  243.3 1.3 pad_maximum_fusion
  244.6 1.9 collective-permute-start
  246.5 2.3 copy.26
  248.8 2.3 copy.31
  251.1 2.6 multiply_convert_fusion.6
  253.7 1.1 multiply_convert_fusion.4
  254.8 87.4 %all_gather.29 = bf16[1024,256]{1,0:T(8,128)(2,1)} all-gather(bf16[256,256]{1,0:T(8,128)(2,1)S(1)} %pad_maximum_fusion.7), channel_id=1, replica_groups=mesh['pipe'=64,'dp'=4] {'dp'}, dimensions={0}, use_global_device_ids=true | all-gather | bytes 655360 | tf_op jit(solution)/shard_map/all_gather | solution.py:138
  342.2 2.1 slice.38
  344.2 2.3 copy.34
  346.5 2.7 pad_maximum_fusion.3
  349.3 4.3 all-to-all-start.1
  353.6 45.2 %all_gather.31 = bf16[1024,256]{1,0:T(8,128)(2,1)} all-gather(bf16[256,256]{1,0:T(8,128)(2,1)S(1)} %pad_maximum_fusion.9), channel_id=1, replica_groups=mesh['pipe'=64,'dp'=4] {'dp'}, dimensions={0}, use_global_device_ids=true | all-gather | bytes 655360 | tf_op jit(solution)/shard_map/all_gather | solution.py:140
  398.8 2.1 slice.39
  400.9 2.3 copy.35
  403.2 2.4 fusion.98
  405.7 1.9 fusion.92
  407.7 1.3 pad_maximum_fusion.5
  409.0 16.5 %all_gather.28 = bf16[1024,256]{1,0:T(8,128)(2,1)} all-gather(bf16[256,256]{1,0:T(8,128)(2,1)S(1)} %pad_maximum_fusion.6), channel_id=1, replica_groups=mesh['pipe'=64,'dp'=4] {'dp'}, dimensions={0}, use_global_device_ids=true | all-gather | bytes 655360 | tf_op jit(solution)/shard_map/all_gather | solution.py:137
  425.6 0.8 multiply_reduce_fusion
  426.3 2.8 fusion.115
  429.2 4.5 all-to-all-start.3
  433.7 43.1 %all_gather.30 = bf16[1024,256]{1,0:T(8,128)(2,1)} all-gather(bf16[256,256]{1,0:T(8,128)(2,1)S(1)} %pad_maximum_fusion.8), channel_id=1, replica_groups=mesh['pipe'=64,'dp'=4] {'dp'}, dimensions={0}, use_global_device_ids=true | all-gather | bytes 655360 | tf_op jit(solution)/shard_map/all_gather | solution.py:139
  476.8 0.7 multiply_reduce_fusion.1
  477.5 2.8 fusion.112
  480.3 3.9 fusion.6
  484.3 3.9 fusion.4
  488.2 2.8 fusion.64
  491.0 2.8 fusion.66
  493.8 1.7 copy.28
  495.5 1.7 copy.33
  497.3 2.5 fusion.65
  499.7 1.4 fusion.67
  (84 shorter events, 3.5 us)
Async XLA Ops:
  7.2 4.2 copy-start.1
  7.2 47.3 %all-gather.5.cloned.1.call-start = ((), (), s32[]{:S(2)}) async-start(), calls=%async_computation.4 | async-start | bytes 1966080 | tf_op jit(solution)/shard_map/all_gather | solution.py:79
  7.9 89.5 %all-gather.7.cloned.1.call-start = ((), (), s32[]{:S(2)}) async-start(), calls=%async_computation.5 | async-start | bytes 1966080 | tf_op jit(solution)/shard_map/all_gather | solution.py:80
  8.7 154.1 %all-gather.9.cloned.1.call-start = ((), (), s32[]{:S(2)}) async-start(), calls=%async_computation.6 | async-start | bytes 1966080 | tf_op jit(solution)/shard_map/all_gather | solution.py:82
  9.4 202.3 %all-gather.11.cloned.1.call-start = ((), (), s32[]{:S(2)}) async-start(), calls=%async_computation.7 | async-start | bytes 1966080 | tf_op jit(solution)/shard_map/all_gather | solution.py:81
  11.3 2.0 copy-start
  13.6 2.0 copy-start.12
  13.6 2.3 copy-start.11
  27.9 2.8 copy-start.10
  97.4 2.4 copy-start.2
  99.8 2.0 copy-start.9
  101.8 1.1 copy-start.14
  104.2 132.5 %all-to-all-start = ((bf16[256,4,768]{2,0,1:T(8,128)(2,1)}), bf16[256,4,768]{2,0,1:T(8,128)(2,1)}, u32[]{:S(2)}, u32[]{:S(2)}) async-start(bf16[256,4,768]{2,0,1:T(8,128)(2,1)} %pad_maximum_fusion.2), calls=%async_computation | async-start | bytes 3145728 | tf_op jit(solution)/shard_map/all_to_all | solution.py:131
  216.0 11.0 %copy-start.4 = (bf16[1,3072,256]{2,1,0:T(8,128)(2,1)S(1)}, bf16[1,3072,256]{2,1,0:T(8,128)(2,1)}, u32[]{:S(2)}) copy-start(bf16[1,3072,256]{2,1,0:T(8,128)(2,1)} %all-gather.11.cloned.1.call-done) | copy-start | bytes 4718596
  218.8 8.7 %copy-start.16 = (bf16[1,128,3072]{2,1,0:T(8,128)(2,1)S(1)}, bf16[1,128,3072]{2,1,0:T(8,128)(2,1)}, u32[]{:S(2)}) copy-start(bf16[1,128,3072]{2,1,0:T(8,128)(2,1)} %param.13) | copy-start | bytes 2359300
  218.8 8.7 %copy-start.20 = (bf16[1,256,3072]{2,1,0:T(8,128)(2,1)S(1)}, bf16[1,256,3072]{2,1,0:T(8,128)(2,1)}, u32[]{:S(2)}) copy-start(bf16[1,256,3072]{2,1,0:T(8,128)(2,1)} %all-gather.9.cloned.1.call-done) | copy-start | bytes 4718596
  218.8 123.4 %collective-permute-start.1 = (bf16[2,128,3072]{2,1,0:T(8,128)(2,1)}, bf16[2,128,3072]{2,1,0:T(8,128)(2,1)}, u32[]{:S(2)}, u32[]{:S(2)}) collective-permute-start(bf16[2,128,3072]{2,1,0:T(8,128)(2,1)} %pad_maximum_fusion.1), channel_id=1, source_target_pairs={{4,0},{8,4},{12,8},{16,12},{20,16},{24,20},{28,24},{32,28},{36,32}... | collective-permute-start | bytes 4718600 | tf_op jit(solution)/shard_map/ppermute | solution.py:12
  228.1 1.9 copy-start.8
  230.0 1.1 copy-start.13
  236.8 112.5 %all-to-all-start.2 = ((bf16[256,4,768]{2,0,1:T(8,128)(2,1)}), bf16[256,4,768]{2,0,1:T(8,128)(2,1)}, u32[]{:S(2)}, u32[]{:S(2)}) async-start(bf16[256,4,768]{2,0,1:T(8,128)(2,1)} %pad_maximum_fusion.4), calls=%async_computation.2 | async-start | bytes 3145728 | tf_op jit(solution)/shard_map/all_to_all | solution.py:133
  241.1 2.2 copy-start.15
  244.6 154.2 %collective-permute-start = (bf16[2,128,3072]{2,1,0:T(8,128)(2,1)}, bf16[2,128,3072]{2,1,0:T(8,128)(2,1)}, u32[]{:S(2)}, u32[]{:S(2)}) collective-permute-start(bf16[2,128,3072]{2,1,0:T(8,128)(2,1)} %pad_maximum_fusion), channel_id=1, source_target_pairs={{0,4},{4,8},{8,12},{12,16},{16,20},{20,24},{24,28},{28,32},{32,36}... | collective-permute-start | bytes 4718600 | tf_op jit(solution)/shard_map/ppermute | solution.py:12
  251.1 2.6 copy-start.5
  349.3 79.9 %all-to-all-start.1 = ((bf16[256,4,768]{0,2,1:T(8,128)(2,1)}), bf16[256,4,768]{0,2,1:T(8,128)(2,1)}, u32[]{:S(2)}, u32[]{:S(2)}) async-start(bf16[256,4,768]{0,2,1:T(8,128)(2,1)} %pad_maximum_fusion.3), calls=%async_computation.1 | async-start | bytes 3145728 | tf_op jit(solution)/shard_map/all_to_all | solution.py:132
  398.8 4.4 copy-start.24
  403.2 2.5 copy-start.21
  403.2 2.5 copy-start.25
  405.7 2.0 copy-start.17
  405.7 2.0 copy-start.18
  407.7 17.9 %copy-start.6 = (bf16[1,3072,256]{2,1,0:T(8,128)(2,1)S(1)}, bf16[1,3072,256]{2,1,0:T(8,128)(2,1)}, u32[]{:S(2)}) copy-start(bf16[1,3072,256]{2,1,0:T(8,128)(2,1)} %all-gather.11.cloned.1.call-done) | copy-start | bytes 4718596
  429.2 47.6 %copy-start.3 = (bf16[1,3072,256]{2,1,0:T(8,128)(2,1)S(1)}, bf16[1,3072,256]{2,1,0:T(8,128)(2,1)}, u32[]{:S(2)}) copy-start(bf16[1,3072,256]{2,1,0:T(8,128)(2,1)} %all-gather.5.cloned.1.call-done) | copy-start | bytes 4718596
  429.2 66.4 %all-to-all-start.3 = ((bf16[256,4,768]{0,2,1:T(8,128)(2,1)}), bf16[256,4,768]{0,2,1:T(8,128)(2,1)}, u32[]{:S(2)}, u32[]{:S(2)}) async-start(bf16[256,4,768]{0,2,1:T(8,128)(2,1)} %pad_maximum_fusion.5), calls=%async_computation.3 | async-start | bytes 3145728 | tf_op jit(solution)/shard_map/all_to_all | solution.py:134
  480.3 4.0 copy-start.7
  484.3 3.9 copy-start.22
  488.2 2.8 copy-start.23
  497.3 2.5 copy-start.19
Sparse Core Ops, SparseCore 0:
  9.8 44.5 all-gather.4
  56.3 41.0 all-gather.6
  99.2 63.4 all-gather.8
  164.4 47.2 all-gather.10
where the time goes:
time: 509 us; the launch traced here: 508 us
  blocking collectives  192 us (38%)
  waiting for transfers between devices  166 us (33%)
  matrix products  44.6 us (9%)
  other arithmetic  32.7 us (6%)
  local copies, waits for them, and re-layouts  30 us (6%)
  starting transfers between devices  27.8 us (5%)
  between operations  14.2 us (3%)
    all_gather x1, blocking collectives, body(): lax.all_gather(joined[0][3], 'dp', axis=0, tiled=True)  87.4 us
    all_gather x1, waiting for transfers between devices, body(): lax.all_gather(mirror_up, 'dp', axis=2, tiled=True)  51.1 us
    all_gather x1, waiting for transfers between devices, body(): lax.all_gather(mirror_down, 'dp', axis=1, tiled=True)  49 us
    all_gather x1, blocking collectives, body(): lax.all_gather(joined[1][3], 'dp', axis=0, tiled=True)  45.2 us
    all_gather x1, blocking collectives, body(): lax.all_gather(joined[1][2], 'dp', axis=0, tiled=True)  43.1 us
    all_gather x1, waiting for transfers between devices, body(): lax.all_gather(lead_up, 'dp', axis=2, tiled=True)  41.1 us
    all_gather x1, waiting for transfers between devices, body(): lax.all_gather(lead_down, 'dp', axis=1, tiled=True)  22.5 us
    all_gather x1, blocking collectives, body(): lax.all_gather(joined[0][2], 'dp', axis=0, tiled=True)  16.5 us
  transfers between devices with their start and end apart: 10, of which 4 were waited for; matrix products, arithmetic and copies ran while one was open for 20% of the time, Pallas kernels for 0%

commit v1 on v0

v1 whole, which is shorter than its diff:
```python
import functools

import jax
import jax.numpy as jnp
from jax import lax
from jax.experimental import pallas as pl
from jax.experimental.pallas import tpu as pltpu
from jax.sharding import PartitionSpec as P

EPS = 1e-06
MESH = pl.DeviceIdType.MESH
BF16 = jnp.bfloat16
F32 = jnp.float32
NT = (((1,), (1,)), ((), ()))


def dot(a, b):
    return jnp.dot(a, b, preferred_element_type=F32)


def dot_nt(a, b):
    return lax.dot_general(a, b, NT, preferred_element_type=F32)


def kernel(
    lf, mf, lg, mg, ls, ms, ld, lu, md, mu,
    o_lf, o_mf, o_lb, o_mb, o_ld, o_lu, o_md, o_mu,
    wd, wu, sv, svt, sc, gb, xb, yb, bb, ob, dl, at, rsd, rsu, gsd, gsu,
    in_sem, out_sem, ag_s, ag_r, pp_s, pp_r, rs_s, rs_r,
):
    p, d = lax.axis_index("pipe"), lax.axis_index("dp")
    stages = lax.axis_size("pipe")
    _, _, rows, width = sv.shape
    shard = wd.shape[2]
    tile = min(256, shard)
    subs = shard // tile
    fronts, grads, saved = (lf, mf), (lg, mg), (ls, ms)
    downs, ups = (ld, md), (lu, mu)
    has_up, has_down = p < stages - 1, p > 0
    has_right, has_left = d < 3, d > 0
    is_end = (d == 0) | (d == 3)
    is_mid = (d == 1) | (d == 2)

    def local(src, dst, n):
        return pltpu.make_async_copy(src, dst, in_sem.at[n])

    loads = {}
    for m in range(2):
        loads["s", m] = local(saved[m].at[0], sv.at[m], m)
        loads["wd", m] = local(downs[m].at[0], wd.at[m, d], 2 + m)
        loads["wu", m] = local(ups[m].at[0], wu.at[m, d], 4 + m)
        loads["g", m] = local(grads[m].at[0], gb.at[m, pl.ds(0, rows)], 6 + m)
        loads["x", m] = local(fronts[m].at[0], xb.at[m, 0], 8 + m)
    for copy in loads.values():
        copy.start()

    barrier = pltpu.get_barrier_semaphore()
    around = (
        (has_up, (p + 1, d)),
        (has_down, (p - 1, d)),
        (has_right, (p, d + 1)),
        (has_left, (p, d - 1)),
    )
    for here, where in around:

        @pl.when(here)
        def _(where=where):
            pl.semaphore_signal(barrier, inc=1, device_id=where, device_id_type=MESH)

    pl.semaphore_wait(barrier, sum(here.astype(jnp.int32) for here, _ in around))

    def ag_copy(m, f, k, kind):
        index = jnp.clip(d - k if f == 0 else d + k, 0, 3)
        whole = (wd, wu)[kind]
        own = (downs, ups)[kind][m]
        return pltpu.make_async_remote_copy(
            src_ref=own.at[0] if k == 0 else whole.at[m, index],
            dst_ref=whole.at[m, index],
            send_sem=ag_s.at[f, m, kind, k],
            recv_sem=ag_r.at[f, m, kind, k],
            device_id=(p, d + 1 if f == 0 else d - 1),
            device_id_type=MESH,
        )

    def ag_sends(f, k):
        return has_right & (d >= k) if f == 0 else has_left & (d + k <= 3)

    def ag_send(m, f, k, here):
        @pl.when(here & ag_sends(f, k))
        def _():
            for kind in range(2):
                ag_copy(m, f, k, kind).start()

    def ag_arrived(m, f, k):
        index = jnp.clip(d - 1 - k if f == 0 else d + 1 + k, 0, 3)
        for kind in range(2):
            whole = (wd, wu)[kind]
            pltpu.make_async_remote_copy(
                src_ref=whole.at[m, index],
                dst_ref=whole.at[m, index],
                send_sem=ag_s.at[f, m, kind, k],
                recv_sem=ag_r.at[f, m, kind, k],
                device_id=(p, d + 1 if f == 0 else d - 1),
                device_id_type=MESH,
            ).wait_recv()

    def ag_forward(m, f, k):
        @pl.when(ag_sends(f, k))
        def _():
            ag_arrived(m, f, k - 1)
            for kind in range(2):
                ag_copy(m, f, k, kind).start()

    def ag_ends(m):
        for f, last in ((0, 3), (1, 0)):

            @pl.when(d == last)
            def _(f=f):
                for k in range(3):
                    ag_arrived(m, f, k)

    def columns(o, s):
        return pl.ds(pl.multiple_of(o * shard + s * tile, tile), tile)

    def block(o):
        return pl.ds(pl.multiple_of(o * shard, shard), shard)

    def scale_of(ref):
        def add(o, total):
            for s in range(subs):
                x = ref[:, columns(o, s)].astype(F32)
                total = total + x * x
            return total

        total = lax.fori_loop(0, 4, add, jnp.zeros((rows, tile), F32))
        return lax.rsqrt(jnp.sum(total, axis=1, keepdims=True) / width + EPS)

    def prepare(m, t):
        ref = sv.at[m, t]
        factor = scale_of(ref)
        sc[m, t] = jnp.broadcast_to(factor, (rows, 128))

        def step(o, carry):
            for s in range(subs):
                here = columns(o, s)
                normed = ref[:, here].astype(F32) * factor
                ref[:, here] = normed.astype(BF16)
                svt[m, here, t * rows : (t + 1) * rows] = normed.T.astype(BF16)
            return carry

        lax.fori_loop(0, 4, step, 0)

    def forward(m, t, out):
        ref = xb.at[m, t]
        factor = scale_of(ref)

        def down(o, total):
            for s in range(subs):
                normed = (ref[:, columns(o, s)].astype(F32) * factor).astype(BF16)
                total = total + dot(normed, wd[m, o, s * tile : (s + 1) * tile, :])
            return total

        latent = lax.fori_loop(0, 4, down, jnp.zeros((rows, wd.shape[3]), F32))
        active = (latent * jax.nn.sigmoid(latent)).astype(BF16)

        def up(o, carry):
            for s in range(subs):
                here = columns(o, s)
                branch = dot(active, wu[m, o, :, s * tile : (s + 1) * tile])
                out[:, here] = (ref[:, here].astype(F32) + branch).astype(BF16)
            return carry

        lax.fori_loop(0, 4, up, 0)

    def backward(m, t, out):
        ref = sv.at[m, t]
        incoming = gb.at[m, pl.ds(t * rows, rows)]
        zero = jnp.zeros((rows, wd.shape[3]), F32)

        def down(o, total):
            latent, d_active = total
            latent = latent + dot(ref[:, block(o)], wd[m, o])
            d_active = d_active + dot_nt(incoming[:, block(o)], wu[m, o])
            return latent, d_active

        latent, d_active = lax.fori_loop(0, 4, down, (zero, zero))
        squash = jax.nn.sigmoid(latent)
        active = latent * squash
        d_latent = (d_active * squash * (1.0 + latent * (1.0 - squash))).astype(BF16)
        dl[m, t * rows : (t + 1) * rows, :] = d_latent
        at[m, :, t * rows : (t + 1) * rows] = active.T.astype(BF16)
        inner = jnp.sum(d_latent.astype(F32) * latent, axis=1, keepdims=True) / width
        factor = sc[m, t][:, 0:1]

        def up(o, carry):
            for s in range(subs):
                here = columns(o, s)
                d_normed = dot_nt(d_latent, wd[m, o, s * tile : (s + 1) * tile, :])
                scaled = ref[:, here].astype(F32)
                out[:, here] = (
                    incoming[:, here].astype(F32) + factor * (d_normed - scaled * inner)
                ).astype(BF16)
            return carry

        lax.fori_loop(0, 4, up, 0)

    def pipe_copy(n):
        m = n % 2
        src = yb.at[m] if n < 2 else bb.at[m]
        dst = xb.at[m, 1] if n < 2 else gb.at[m, pl.ds(rows, rows)]
        return pltpu.make_async_remote_copy(
            src_ref=src,
            dst_ref=dst,
            send_sem=pp_s.at[n],
            recv_sem=pp_r.at[n],
            device_id=(p + 1 if n in (0, 3) else p - 1, d),
            device_id_type=MESH,
        )

    def pipe_ends(n):
        return (has_up, has_down) if n in (0, 3) else (has_down, has_up)

    def pipe_send(n):
        @pl.when(pipe_ends(n)[0])
        def _():
            pipe_copy(n).start()

    def pipe_wait(n):
        arrives = pipe_ends(n)[1]

        @pl.when(arrives)
        def _():
            pipe_copy(n).wait_recv()

        @pl.when(jnp.logical_not(arrives))
        def _():
            m = n % 2
            if n < 2:
                xb[m, 1] = jnp.zeros((rows, width), BF16)
            else:
                gb[m, rows : 2 * rows, :] = jnp.zeros((rows, width), BF16)

    def rs_copy(m, f, j, kind, target):
        held = (rsd, rsu)[kind]
        return pltpu.make_async_remote_copy(
            src_ref=held.at[f, m, j],
            dst_ref=held.at[f, m, j],
            send_sem=rs_s.at[f, m, j, kind],
            recv_sem=rs_r.at[f, m, j, kind],
            device_id=(p, target),
            device_id_type=MESH,
        )

    def piece(m, o, kind, out, arrived=()):
        for s in range(subs):
            if kind == 0:
                here = (slice(s * tile, (s + 1) * tile), slice(None))
                part = dot(svt[m, columns(o, s), :], dl[m])
            else:
                here = (slice(None), slice(s * tile, (s + 1) * tile))
                part = dot(at[m], gb[m, :, columns(o, s)])
            for ref in arrived:
                part = part + ref[here].astype(F32)
            out[here] = part.astype(BF16)

    flow = jnp.where(d == 0, 0, 1)

    def rs_ends(m, j):
        @pl.when(is_end)
        def _():
            owner = jnp.where(d == 0, 3 - j, j)
            for kind in range(2):
                piece(m, owner, kind, (rsd, rsu)[kind].at[flow, m, j])
                rs_copy(m, flow, j, kind, jnp.where(d == 0, 1, 2)).start()

    def rs_passes(f, j):
        return is_mid & ((d < 3 - j) if f == 0 else (d > j))

    def rs_mids(m):
        for j in range(2):
            for kind in range(2):
                for f in range(2):

                    @pl.when(rs_passes(f, j))
                    def _(j=j, kind=kind, f=f):
                        copy = rs_copy(m, f, j, kind, d + 1 if f == 0 else d - 1)
                        copy.wait_recv()
                        held = (rsd, rsu)[kind].at[f, m, j]
                        piece(m, 3 - j if f == 0 else j, kind, held, (held,))
                        copy.start()

    def rs_finish(m):
        for kind in range(2):
            held, out = (rsd, rsu)[kind], (gsd, gsu)[kind].at[m]

            @pl.when(is_end)
            def _():
                rs_copy(m, 1 - flow, 0, kind, jnp.where(d == 0, 1, 2)).wait_recv()
                piece(m, d, kind, out, (held.at[1 - flow, m, 0],))

            @pl.when(is_mid)
            def _():
                rs_copy(m, 0, 3 - d, kind, d + 1).wait_recv()
                rs_copy(m, 1, d, kind, d - 1).wait_recv()
                piece(m, d, kind, out, (held.at[0, m, 3 - d], held.at[1, m, d]))

    results = (
        (ob.at[0], o_lf), (ob.at[1], o_mf), (ob.at[2], o_lb), (ob.at[3], o_mb),
        (gsd.at[0], o_ld), (gsu.at[0], o_lu), (gsd.at[1], o_md), (gsu.at[1], o_mu),
    )

    def result(n):
        return pltpu.make_async_copy(results[n][0], results[n][1].at[0], out_sem.at[n])

    everyone = d >= 0
    for f in range(2):
        ag_send(0, f, 0, everyone)
    for m in range(2):
        loads["s", m].wait()
        for t in range(2):
            prepare(m, t)
    for key in ("wd", "wu", "g", "x"):
        for m in range(2):
            loads[key, m].wait()
    for f in range(2):
        ag_forward(0, f, 1)
        ag_send(1, f, 0, d == (0, 3)[f])
    for f in range(2):
        ag_forward(0, f, 2)
        ag_send(1, f, 0, d == (1, 2)[f])
    ag_ends(0)

    backward(0, 0, bb.at[0])
    pipe_send(2)
    for f in range(2):
        ag_send(1, f, 0, d == (2, 1)[f])
    forward(0, 0, yb.at[0])
    pipe_send(0)

    for f in range(2):
        ag_forward(1, f, 1)
    for f in range(2):
        ag_forward(1, f, 2)

    pipe_wait(2)
    backward(0, 1, ob.at[2])
    result(2).start()
    rs_ends(0, 0)
    rs_ends(0, 1)
    pipe_wait(0)
    forward(0, 1, ob.at[0])
    result(0).start()

    ag_ends(1)
    backward(1, 0, bb.at[1])
    pipe_send(3)
    rs_ends(0, 2)
    forward(1, 0, yb.at[1])
    pipe_send(1)

    pipe_wait(3)
    backward(1, 1, ob.at[3])
    result(3).start()
    rs_ends(1, 0)
    rs_ends(1, 1)
    rs_ends(1, 2)
    rs_mids(0)
    pipe_wait(1)
    forward(1, 1, ob.at[1])
    result(1).start()
    rs_finish(0)
    result(4).start()
    result(5).start()
    rs_mids(1)
    rs_finish(1)
    result(6).start()
    result(7).start()

    for m in range(2):
        for f in range(2):
            for k in range(3):

                @pl.when(ag_sends(f, k))
                def _(m=m, f=f, k=k):
                    for kind in range(2):
                        ag_copy(m, f, k, kind).wait_send()

    for n in range(4):

        @pl.when(pipe_ends(n)[0])
        def _(n=n):
            pipe_copy(n).wait_send()

    for m in range(2):

        @pl.when(is_end)
        def _(m=m):
            for j in range(3):
                for kind in range(2):
                    rs_copy(m, flow, j, kind, jnp.where(d == 0, 1, 2)).wait_send()

        for j in range(2):
            for f in range(2):

                @pl.when(rs_passes(f, j))
                def _(m=m, j=j, f=f):
                    for kind in range(2):
                        rs_copy(m, f, j, kind, d + 1 if f == 0 else d - 1).wait_send()

    for n in range(8):
        result(n).wait()


def body(*arrays):
    lf, ls, ld, lu = arrays[0], arrays[4], arrays[6], arrays[7]
    _, ticks, rows, width = ls.shape
    _, shard, latents = ld.shape
    outs = [jax.ShapeDtypeStruct(lf.shape, BF16)] * 4 + [
        jax.ShapeDtypeStruct(ld.shape, BF16),
        jax.ShapeDtypeStruct(lu.shape, BF16),
    ] * 2
    vmem = pltpu.VMEM
    dma = pltpu.SemaphoreType.DMA
    return pl.pallas_call(
        kernel,
        out_shape=outs,
        in_specs=[pl.BlockSpec(memory_space=pl.ANY)] * 10,
        out_specs=[pl.BlockSpec(memory_space=pl.ANY)] * 8,
        scratch_shapes=[
            vmem((2, 4, shard, latents), BF16),
            vmem((2, 4, latents, shard), BF16),
            vmem((2, ticks, rows, width), BF16),
            vmem((2, width, ticks * rows), BF16),
            vmem((2, ticks, rows, 128), F32),
            vmem((2, ticks * rows, width), BF16),
            vmem((2, ticks, rows, width), BF16),
            vmem((2, rows, width), BF16),
            vmem((2, rows, width), BF16),
            vmem((4, rows, width), BF16),
            vmem((2, ticks * rows, latents), BF16),
            vmem((2, latents, ticks * rows), BF16),
            vmem((2, 2, 3, shard, latents), BF16),
            vmem((2, 2, 3, latents, shard), BF16),
            vmem((2, shard, latents), BF16),
            vmem((2, latents, shard), BF16),
            dma((10,)),
            dma((8,)),
            dma((2, 2, 2, 3)),
            dma((2, 2, 2, 3)),
            dma((4,)),
            dma((4,)),
            dma((2, 2, 3, 2)),
            dma((2, 2, 3, 2)),
        ],
        compiler_params=pltpu.CompilerParams(
            collective_id=0, has_side_effects=True, vmem_limit_bytes=52 * 2**20
        ),
        name="relay_window",
    )(*arrays)


def solution(mesh):
    front = P("pipe", "dp", None)
    up = P("pipe", None, "dp")
    placed = (front,) * 4 + (P("pipe", None, "dp", None),) * 2 + (front, up, front, up)
    return jax.shard_map(
        body,
        mesh=mesh,
        in_specs=placed,
        out_specs=(front,) * 4 + (front, up, front, up),
        check_vma=False,
    )
```

time: 509 us -> 293 us (0.58)
  Pallas kernels: 0 us -> 278 us
  blocking collectives: 192 us -> 0 us
  waiting for transfers between devices: 166 us -> 0 us
  matrix products: 44.6 us -> 0 us
  other arithmetic: 32.7 us -> 0 us
  starting transfers between devices: 27.8 us -> 0 us
  local copies, waits for them, and re-layouts: 30 us -> 8.8 us
  between operations: 14.2 us -> 0.67 us
    pallas_call x0 -> x1, Pallas kernels: none -> 278 us  [body(): pl.pallas_call(kernel, out_shape=outs, in_specs=[pl.BlockSpec(memory_spac...]
    all_gather x4 -> x0, blocking collectives: 192 us -> none  [the longest x1 87.4 us: body(): lax.all_gather(joined[0][3], 'dp', axis=0, tiled=True)]
    all_gather x4 -> x0, waiting for transfers between devices: 164 us -> none  [the longest x1 51.1 us: body(): lax.all_gather(mirror_up, 'dp', axis=2, tiled=True)]
    dot_general x20 -> x0, matrix products: 44.6 us -> none  [the longest x4 16.4 us: section_forward(): jnp.dot(active, w_up, preferred_element_type=jnp.float32)]
    all_to_all x4 -> x0, starting transfers between devices: 17.6 us -> none  [the longest x1 4.49 us: body(): lax.all_to_all(joined[1][1], 'dp', split_axis=1, concat_axis=0, tiled=True)]
    convert_element_type x4 -> x0, local copies, waits for them, and re-layouts: 11.7 us -> none  [normalize(): float_in = inputs.astype(jnp.float32)]
    ppermute x2 -> x0, starting transfers between devices: 10.1 us -> none  [passed_along(): lax.ppermute(value, axis, [(source, source + steps) for source in range(i...]
    another operation x4 -> x0, other arithmetic: 9.31 us -> none  [the longest x2 5.85 us: body(): behind = send_downward(jnp.stack([produced[1], returned[0]]))]
  transfers between devices with their start and end apart: 10 -> 0, of which waited for: 4 -> 0; matrix products, arithmetic and copies ran while one was open for 20% -> 0% of each run, Pallas kernels for 0% -> 0%
where the time goes in v1:
time: 293 us; the launch traced here: 288 us
  Pallas kernels  278 us (95%)
  local copies, waits for them, and re-layouts  8.8 us (3%)
    pallas_call x1, Pallas kernels, body(): pl.pallas_call(kernel, out_shape=outs, in_specs=[pl.BlockSpec(memory_spac...  278 us
    unnamed x16, local copies, waits for them, and re-layouts  8.8 us

profile of v1, /device:TPU:6, one launch (start us, length us, event | category | flops | bytes accessed | tf_op | source)
XLA Modules:
  0.0 287.7 jit_solution(3390608751406847358)
XLA Ops:
  0.6 0.0 copy-start
  0.6 1.0 copy-done
  1.6 278.2 %relay_window.1 = (bf16[1,128,3072]{2,1,0:T(8,128)(2,1)}, bf16[1,128,3072]{2,1,0:T(8,128)(2,1)}, bf16[1,128,3072]{2,1,0:T(8,128)(2,1)}, bf16[1,128,3072]{2,1,0:T...) custom-call(bf16[1,128,3072]{2,1,0:T(8,128)(2,1)} %lf.1, ...), custom_call_target="tpu_custom_call" | custom-call | tf_op jit(solution)/shard_map/relay_window/pallas_call | solution.py:424
  279.9 0.0 copy-start.3
  279.9 0.0 copy-start.2
  279.9 2.2 copy.26
  282.1 0.0 copy-done.3
  282.1 0.0 copy-start.1
  282.1 0.9 copy.27
  283.0 0.0 copy-done.2
  283.0 0.9 copy.28
  283.8 0.0 copy-done.1
  283.8 0.9 copy.29
  284.7 0.7 copy.30
  285.5 0.7 copy.31
  286.2 0.7 copy.32
  287.0 0.7 copy.33
Async XLA Ops:
  0.6 1.0 copy-start
  279.9 2.2 copy-start.3
  279.9 3.1 %copy-start.2 = (bf16[1,128,3072]{2,1,0:T(8,128)(2,1)S(1)}, bf16[1,128,3072]{2,1,0:T(8,128)(2,1)}, u32[]{:S(2)}) copy-start(bf16[1,128,3072]{2,1,0:T(8,128)(2,1)} %get-tuple-element.18) | copy-start | bytes 2359300
  282.1 1.8 copy-start.1

commit v2 on v1

--- a/solution.py
+++ b/solution.py
@@ -69,55 +69,57 @@
 
     pl.semaphore_wait(barrier, sum(here.astype(jnp.int32) for here, _ in around))
 
-    def ag_copy(m, f, k, kind):
-        index = jnp.clip(d - k if f == 0 else d + k, 0, 3)
+    out_to, out_flow = jnp.where(d == 0, 1, 2), jnp.where(d == 0, 0, 1)
+    cross_to, cross_flow = 3 - d, jnp.clip(d - 1, 0, 1)
+    end_to, end_flow = jnp.where(d == 1, 0, 3), jnp.clip(2 - d, 0, 1)
+
+    def ag_copy(m, kind, flow, step, shard_of, target, own=False):
         whole = (wd, wu)[kind]
-        own = (downs, ups)[kind][m]
         return pltpu.make_async_remote_copy(
-            src_ref=own.at[0] if k == 0 else whole.at[m, index],
-            dst_ref=whole.at[m, index],
-            send_sem=ag_s.at[f, m, kind, k],
-            recv_sem=ag_r.at[f, m, kind, k],
-            device_id=(p, d + 1 if f == 0 else d - 1),
+            src_ref=(downs, ups)[kind][m].at[0] if own else whole.at[m, shard_of],
+            dst_ref=whole.at[m, shard_of],
+            send_sem=ag_s.at[flow, m, kind, step],
+            recv_sem=ag_r.at[flow, m, kind, step],
+            device_id=(p, target),
             device_id_type=MESH,
         )
 
-    def ag_sends(f, k):
-        return has_right & (d >= k) if f == 0 else has_left & (d + k <= 3)
-
-    def ag_send(m, f, k, here):
-        @pl.when(here & ag_sends(f, k))
-        def _():
-            for kind in range(2):
-                ag_copy(m, f, k, kind).start()
-
-    def ag_arrived(m, f, k):
-        index = jnp.clip(d - 1 - k if f == 0 else d + 1 + k, 0, 3)
-        for kind in range(2):
-            whole = (wd, wu)[kind]
-            pltpu.make_async_remote_copy(
-                src_ref=whole.at[m, index],
-                dst_ref=whole.at[m, index],
-                send_sem=ag_s.at[f, m, kind, k],
-                recv_sem=ag_r.at[f, m, kind, k],
-                device_id=(p, d + 1 if f == 0 else d - 1),
-                device_id_type=MESH,
-            ).wait_recv()
-
-    def ag_forward(m, f, k):
-        @pl.when(ag_sends(f, k))
-        def _():
-            ag_arrived(m, f, k - 1)
-            for kind in range(2):
-                ag_copy(m, f, k, kind).start()
-
-    def ag_ends(m):
-        for f, last in ((0, 3), (1, 0)):
-
-            @pl.when(d == last)
-            def _(f=f):
-                for k in range(3):
-                    ag_arrived(m, f, k)
+    def own_from_end(m, kind):
+        @pl.when(is_end)
+        def _():
+            ag_copy(m, kind, out_flow, 0, d, out_to, True).start()
+
+    def own_across(m, kind):
+        @pl.when(is_mid)
+        def _():
+            ag_copy(m, kind, cross_flow, 0, d, cross_to, True).start()
+
+    def own_to_end(m, kind):
+        @pl.when(is_mid)
+        def _():
+            ag_copy(m, kind, end_flow, 0, d, end_to, True).start()
+
+    def pass_across(m, kind):
+        @pl.when(is_mid)
+        def _():
+            ag_copy(m, kind, cross_flow, 0, end_to, cross_to).wait_recv()
+            ag_copy(m, kind, cross_flow, 1, end_to, cross_to).start()
+
+    def pass_to_end(m, kind, step):
+        shard_of = cross_to if step == 1 else 3 - end_to
+
+        @pl.when(is_mid)
+        def _():
+            ag_copy(m, kind, end_flow, step - 1, shard_of, end_to).wait_recv()
+            ag_copy(m, kind, end_flow, step, shard_of, end_to).start()
+
+    def end_gathers(m):
+        @pl.when(is_end)
+        def _():
+            for step in range(3):
+                shard_of = jnp.where(d == 0, 1 + step, 2 - step)
+                for kind in range(2):
+                    ag_copy(m, kind, 1 - out_flow, step, shard_of, out_to).wait_recv()
 
     def columns(o, s):
         return pl.ds(pl.multiple_of(o * shard + s * tile, tile), tile)
@@ -220,8 +222,11 @@
     def pipe_ends(n):
         return (has_up, has_down) if n in (0, 3) else (has_down, has_up)
 
-    def pipe_send(n):
-        @pl.when(pipe_ends(n)[0])
+    def pipe_send(n, far):
+        first = lax.rem(p, 2) == 0
+        near = first if n in (0, 3) else jnp.logical_not(first)
+
+        @pl.when(pipe_ends(n)[0] & (jnp.logical_not(near) if far else near))
         def _():
             pipe_copy(n).start()
 
@@ -263,46 +268,48 @@
                 part = part + ref[here].astype(F32)
             out[here] = part.astype(BF16)
 
-    flow = jnp.where(d == 0, 0, 1)
-
-    def rs_ends(m, j):
+    def grad_from_end(m, j, kind):
         @pl.when(is_end)
         def _():
             owner = jnp.where(d == 0, 3 - j, j)
-            for kind in range(2):
-                piece(m, owner, kind, (rsd, rsu)[kind].at[flow, m, j])
-                rs_copy(m, flow, j, kind, jnp.where(d == 0, 1, 2)).start()
-
-    def rs_passes(f, j):
-        return is_mid & ((d < 3 - j) if f == 0 else (d > j))
-
-    def rs_mids(m):
-        for j in range(2):
-            for kind in range(2):
-                for f in range(2):
-
-                    @pl.when(rs_passes(f, j))
-                    def _(j=j, kind=kind, f=f):
-                        copy = rs_copy(m, f, j, kind, d + 1 if f == 0 else d - 1)
-                        copy.wait_recv()
-                        held = (rsd, rsu)[kind].at[f, m, j]
-                        piece(m, 3 - j if f == 0 else j, kind, held, (held,))
-                        copy.start()
-
-    def rs_finish(m):
+            piece(m, owner, kind, (rsd, rsu)[kind].at[out_flow, m, j])
+            rs_copy(m, out_flow, j, kind, out_to).start()
+
+    def grad_across(m, j, kind):
+        @pl.when(is_mid)
+        def _():
+            owner = jnp.where(d == 1, 3 - j, j)
+            copy = rs_copy(m, cross_flow, j, kind, cross_to)
+            copy.wait_recv()
+            held = (rsd, rsu)[kind].at[cross_flow, m, j]
+            piece(m, owner, kind, held, (held,))
+            copy.start()
+
+    def grad_to_end(m, kind):
+        @pl.when(is_mid)
+        def _():
+            copy = rs_copy(m, end_flow, 0, kind, end_to)
+            copy.wait_recv()
+            held = (rsd, rsu)[kind].at[end_flow, m, 0]
+            piece(m, end_to, kind, held, (held,))
+            copy.start()
+
+    def grad_finish(m):
         for kind in range(2):
             held, out = (rsd, rsu)[kind], (gsd, gsu)[kind].at[m]
 
             @pl.when(is_end)
             def _():
-                rs_copy(m, 1 - flow, 0, kind, jnp.where(d == 0, 1, 2)).wait_recv()
-                piece(m, d, kind, out, (held.at[1 - flow, m, 0],))
+                rs_copy(m, 1 - out_flow, 0, kind, out_to).wait_recv()
+                piece(m, d, kind, out, (held.at[1 - out_flow, m, 0],))
 
             @pl.when(is_mid)
             def _():
-                rs_copy(m, 0, 3 - d, kind, d + 1).wait_recv()
-                rs_copy(m, 1, d, kind, d - 1).wait_recv()
-                piece(m, d, kind, out, (held.at[0, m, 3 - d], held.at[1, m, d]))
+                rs_copy(m, cross_flow, 2, kind, cross_to).wait_recv()
+                rs_copy(m, end_flow, 1, kind, end_to).wait_recv()
+                piece(m, d, kind, out, (held.at[cross_flow, m, 2], held.at[end_flow, m, 1]))
+
+            result(4 + 2 * m + kind).start()
 
     results = (
         (ob.at[0], o_lf), (ob.at[1], o_mf), (ob.at[2], o_lb), (ob.at[3], o_mb),
@@ -312,100 +319,120 @@
     def result(n):
         return pltpu.make_async_copy(results[n][0], results[n][1].at[0], out_sem.at[n])
 
-    everyone = d >= 0
-    for f in range(2):
-        ag_send(0, f, 0, everyone)
-    for m in range(2):
-        loads["s", m].wait()
-        for t in range(2):
-            prepare(m, t)
-    for key in ("wd", "wu", "g", "x"):
-        for m in range(2):
-            loads[key, m].wait()
-    for f in range(2):
-        ag_forward(0, f, 1)
-        ag_send(1, f, 0, d == (0, 3)[f])
-    for f in range(2):
-        ag_forward(0, f, 2)
-        ag_send(1, f, 0, d == (1, 2)[f])
-    ag_ends(0)
-
+    own_to_end(0, 1)
+    own_from_end(0, 1)
+    own_across(0, 1)
+    own_to_end(0, 0)
+    own_across(0, 0)
+    pass_to_end(0, 1, 1)
+    pass_across(0, 1)
+    own_from_end(0, 0)
+    loads["s", 0].wait()
+    prepare(0, 0)
+    prepare(0, 1)
+    loads["s", 1].wait()
+    prepare(1, 0)
+    prepare(1, 1)
+    pass_across(0, 0)
+    own_across(1, 0)
+    pass_to_end(0, 0, 1)
+    pass_to_end(0, 1, 2)
+    own_from_end(1, 0)
+    pass_to_end(0, 0, 2)
+    own_from_end(1, 1)
+    loads["wd", 0].wait()
+    loads["wu", 0].wait()
+    loads["g", 0].wait()
+    end_gathers(0)
     backward(0, 0, bb.at[0])
-    pipe_send(2)
-    for f in range(2):
-        ag_send(1, f, 0, d == (2, 1)[f])
-    forward(0, 0, yb.at[0])
-    pipe_send(0)
-
-    for f in range(2):
-        ag_forward(1, f, 1)
-    for f in range(2):
-        ag_forward(1, f, 2)
-
+    pipe_send(2, True)
+    pipe_send(2, False)
     pipe_wait(2)
     backward(0, 1, ob.at[2])
     result(2).start()
-    rs_ends(0, 0)
-    rs_ends(0, 1)
+    grad_from_end(0, 0, 1)
+    grad_from_end(0, 1, 1)
+    grad_from_end(0, 1, 0)
+    pass_across(1, 1)
+    loads["x", 0].wait()
+    forward(0, 0, yb.at[0])
+    pass_across(1, 0)
+    pass_to_end(1, 0, 1)
+    pass_to_end(1, 0, 2)
+    own_to_end(1, 1)
+    grad_across(0, 0, 1)
+    own_across(1, 1)
+    grad_from_end(0, 0, 0)
+    grad_across(0, 1, 0)
+    grad_from_end(0, 2, 1)
+    grad_from_end(0, 2, 0)
+    pass_to_end(1, 1, 1)
+    pass_to_end(1, 1, 2)
+    grad_across(0, 1, 1)
+    own_to_end(1, 0)
+    grad_across(0, 0, 0)
+    loads["wd", 1].wait()
+    loads["wu", 1].wait()
+    loads["g", 1].wait()
+    end_gathers(1)
+    backward(1, 0, bb.at[1])
+    pipe_send(3, True)
+    pipe_send(3, False)
+    loads["x", 1].wait()
+    forward(1, 0, yb.at[1])
+    pipe_send(0, True)
+    pipe_wait(3)
+    backward(1, 1, ob.at[3])
+    result(3).start()
+    grad_across(1, 0, 1)
+    grad_to_end(0, 1)
+    grad_to_end(1, 1)
+    grad_across(1, 0, 0)
+    grad_from_end(1, 0, 1)
+    grad_to_end(0, 0)
+    grad_to_end(1, 0)
+    pipe_send(0, False)
+    grad_from_end(1, 0, 0)
+    grad_from_end(1, 1, 1)
+    grad_across(1, 1, 0)
+    pipe_send(1, False)
+    grad_from_end(1, 1, 0)
+    grad_across(1, 1, 1)
+    pipe_send(1, True)
+    grad_from_end(1, 2, 0)
+    grad_from_end(1, 2, 1)
+    grad_finish(0)
     pipe_wait(0)
     forward(0, 1, ob.at[0])
     result(0).start()
-
-    ag_ends(1)
-    backward(1, 0, bb.at[1])
-    pipe_send(3)
-    rs_ends(0, 2)
-    forward(1, 0, yb.at[1])
-    pipe_send(1)
-
-    pipe_wait(3)
-    backward(1, 1, ob.at[3])
-    result(3).start()
-    rs_ends(1, 0)
-    rs_ends(1, 1)
-    rs_ends(1, 2)
-    rs_mids(0)
     pipe_wait(1)
     forward(1, 1, ob.at[1])
     result(1).start()
-    rs_finish(0)
-    result(4).start()
-    result(5).start()
-    rs_mids(1)
-    rs_finish(1)
-    result(6).start()
-    result(7).start()
+    grad_finish(1)
 
     for m in range(2):
-        for f in range(2):
-            for k in range(3):
-
-                @pl.when(ag_sends(f, k))
-                def _(m=m, f=f, k=k):
-                    for kind in range(2):
-                        ag_copy(m, f, k, kind).wait_send()
+        for kind in range(2):
+
+            @pl.when(is_end)
+            def _(m=m, kind=kind):
+                ag_copy(m, kind, out_flow, 0, d, out_to, True).wait_send()
+                for j in range(3):
+                    rs_copy(m, out_flow, j, kind, out_to).wait_send()
+
+            @pl.when(is_mid)
+            def _(m=m, kind=kind):
+                for step in range(2):
+                    ag_copy(m, kind, cross_flow, step, d, cross_to).wait_send()
+                    rs_copy(m, cross_flow, step, kind, cross_to).wait_send()
+                for step in range(3):
+                    ag_copy(m, kind, end_flow, step, d, end_to).wait_send()
+                rs_copy(m, end_flow, 0, kind, end_to).wait_send()
 
     for n in range(4):
 
         @pl.when(pipe_ends(n)[0])
         def _(n=n):
             pipe_copy(n).wait_send()
-
-    for m in range(2):
-
-        @pl.when(is_end)
-        def _(m=m):
-            for j in range(3):
-                for kind in range(2):
-                    rs_copy(m, flow, j, kind, jnp.where(d == 0, 1, 2)).wait_send()
-
-        for j in range(2):
-            for f in range(2):
-
-                @pl.when(rs_passes(f, j))
-                def _(m=m, j=j, f=f):
-                    for kind in range(2):
-                        rs_copy(m, f, j, kind, d + 1 if f == 0 else d - 1).wait_send()
 
     for n in range(8):
         result(n).wait()

time: 293 us -> 242 us (0.83)
  Pallas kernels: 278 us -> 229 us
    pallas_call x1, Pallas kernels: 278 us -> 229 us  [body(): pl.pallas_call(kernel, out_shape=outs, in_specs=[pl.BlockSpec(memory_spac...]
where the time goes in v2:
time: 242 us; the launch traced here: 238 us
  Pallas kernels  229 us (95%)
  local copies, waits for them, and re-layouts  8.8 us (4%)
    pallas_call x1, Pallas kernels, body(): pl.pallas_call(kernel, out_shape=outs, in_specs=[pl.BlockSpec(memory_spac...  229 us
    unnamed x16, local copies, waits for them, and re-layouts  8.8 us

profile of v2, /device:TPU:6, one launch (start us, length us, event | category | flops | bytes accessed | tf_op | source)
XLA Modules:
  0.0 238.3 jit_solution(17161983512236305864)
XLA Ops:
  0.6 0.0 copy-start
  0.6 1.0 copy-done
  1.6 228.8 %relay_window.1 = (bf16[1,128,3072]{2,1,0:T(8,128)(2,1)}, bf16[1,128,3072]{2,1,0:T(8,128)(2,1)}, bf16[1,128,3072]{2,1,0:T(8,128)(2,1)}, bf16[1,128,3072]{2,1,0:T...) custom-call(bf16[1,128,3072]{2,1,0:T(8,128)(2,1)} %lf.1, ...), custom_call_target="tpu_custom_call" | custom-call | tf_op jit(solution)/shard_map/relay_window/pallas_call | solution.py:451
  230.5 0.0 copy-start.3
  230.5 0.0 copy-start.2
  230.5 2.2 copy.26
  232.7 0.0 copy-done.3
  232.7 0.0 copy-start.1
  232.7 0.9 copy.27
  233.5 0.0 copy-done.2
  233.5 0.9 copy.28
  234.4 0.0 copy-done.1
  234.4 0.9 copy.29
  235.3 0.7 copy.30
  236.1 0.7 copy.31
  236.8 0.7 copy.32
  237.5 0.7 copy.33
Async XLA Ops:
  0.6 1.0 copy-start
  230.5 2.2 copy-start.3
  230.5 3.1 %copy-start.2 = (bf16[1,128,3072]{2,1,0:T(8,128)(2,1)S(1)}, bf16[1,128,3072]{2,1,0:T(8,128)(2,1)}, u32[]{:S(2)}) copy-start(bf16[1,128,3072]{2,1,0:T(8,128)(2,1)} %get-tuple-element.18) | copy-start | bytes 2359300
  232.7 1.8 copy-start.1

commit v3 on v2

--- a/solution.py
+++ b/solution.py
@@ -25,8 +25,8 @@
 def kernel(
     lf, mf, lg, mg, ls, ms, ld, lu, md, mu,
     o_lf, o_mf, o_lb, o_mb, o_ld, o_lu, o_md, o_mu,
-    wd, wu, sv, svt, sc, gb, xb, yb, bb, ob, dl, at, rsd, rsu, gsd, gsu,
-    in_sem, out_sem, ag_s, ag_r, pp_s, pp_r, rs_s, rs_r,
+    wd, wu, sv, svt, sc, gb, xb, yb, bb, ob, dl, at, rsd, rsu, gsd, gsu, far_n, far_dl, far_g, far_at,
+    in_sem, out_sem, ag_s, ag_r, pp_s, pp_r, rs_s, rs_r, op_s, op_r, lt_s, lt_r,
 ):
     p, d = lax.axis_index("pipe"), lax.axis_index("dp")
     stages = lax.axis_size("pipe")
@@ -40,6 +40,7 @@
     has_right, has_left = d < 3, d > 0
     is_end = (d == 0) | (d == 3)
     is_mid = (d == 1) | (d == 2)
+    by_operands = ((), (0,))
 
     def local(src, dst, n):
         return pltpu.make_async_copy(src, dst, in_sem.at[n])
@@ -256,14 +257,65 @@
             device_id_type=MESH,
         )
 
-    def piece(m, o, kind, out, arrived=()):
+    def operand(m, j, which):
+        owner = jnp.where(d == 0, 3 - j, j)
+        half = pl.ds(0 if which == 1 else rows, rows)
+        src, dst = (
+            (svt.at[m, block(owner)], far_n.at[m, j])
+            if which == 0
+            else (gb.at[m, half, block(owner)], far_g.at[m, j, half])
+        )
+        return pltpu.make_async_remote_copy(
+            src_ref=src,
+            dst_ref=dst,
+            send_sem=op_s.at[m, j, which],
+            recv_sem=op_r.at[m, j, which],
+            device_id=(p, out_to),
+            device_id_type=MESH,
+        )
+
+    def latents_copy(m, kind):
+        return pltpu.make_async_remote_copy(
+            src_ref=(dl, at)[kind].at[m],
+            dst_ref=(far_dl, far_at)[kind].at[m],
+            send_sem=lt_s.at[m, kind],
+            recv_sem=lt_r.at[m, kind],
+            device_id=(p, out_to),
+            device_id_type=MESH,
+        )
+
+    def operand_from_end(m, j, which):
+        @pl.when(is_end)
+        def _():
+            operand(m, j, which).start()
+
+    def latents_from_end(m, kind):
+        @pl.when(is_end)
+        def _():
+            latents_copy(m, kind).start()
+
+    def latents_arrive(m):
+        @pl.when(is_mid)
+        def _():
+            for kind in by_operands[m]:
+                latents_copy(m, kind).wait_recv()
+
+    def piece(m, o, kind, out, arrived=(), far=None):
+        if far is not None:
+            for which in ((0,), (1, 2))[kind]:
+                operand(m, far, which).wait_recv()
         for s in range(subs):
+            cut = slice(s * tile, (s + 1) * tile)
             if kind == 0:
-                here = (slice(s * tile, (s + 1) * tile), slice(None))
+                here = (cut, slice(None))
                 part = dot(svt[m, columns(o, s), :], dl[m])
+                if far is not None:
+                    part = part + dot(far_n[m, far, cut, :], far_dl[m])
             else:
-                here = (slice(None), slice(s * tile, (s + 1) * tile))
+                here = (slice(None), cut)
                 part = dot(at[m], gb[m, :, columns(o, s)])
+                if far is not None:
+                    part = part + dot(far_at[m], far_g[m, far, :, cut])
             for ref in arrived:
                 part = part + ref[here].astype(F32)
             out[here] = part.astype(BF16)
@@ -280,9 +332,12 @@
         def _():
             owner = jnp.where(d == 1, 3 - j, j)
             copy = rs_copy(m, cross_flow, j, kind, cross_to)
-            copy.wait_recv()
             held = (rsd, rsu)[kind].at[cross_flow, m, j]
-            piece(m, owner, kind, held, (held,))
+            if kind in by_operands[m]:
+                piece(m, owner, kind, held, (), j)
+            else:
+                copy.wait_recv()
+                piece(m, owner, kind, held, (held,))
             copy.start()
 
     def grad_to_end(m, kind):
@@ -305,9 +360,12 @@
 
             @pl.when(is_mid)
             def _():
-                rs_copy(m, cross_flow, 2, kind, cross_to).wait_recv()
                 rs_copy(m, end_flow, 1, kind, end_to).wait_recv()
-                piece(m, d, kind, out, (held.at[cross_flow, m, 2], held.at[end_flow, m, 1]))
+                if kind in by_operands[m]:
+                    piece(m, d, kind, out, (held.at[end_flow, m, 1],), 2)
+                else:
+                    rs_copy(m, cross_flow, 2, kind, cross_to).wait_recv()
+                    piece(m, d, kind, out, (held.at[cross_flow, m, 2], held.at[end_flow, m, 1]))
 
             result(4 + 2 * m + kind).start()
 
@@ -319,27 +377,32 @@
     def result(n):
         return pltpu.make_async_copy(results[n][0], results[n][1].at[0], out_sem.at[n])
 
+    own_to_end(0, 0)
+    own_from_end(0, 0)
+    own_from_end(0, 1)
     own_to_end(0, 1)
-    own_from_end(0, 1)
+    own_from_end(1, 0)
     own_across(0, 1)
-    own_to_end(0, 0)
+    loads["s", 1].wait()
+    prepare(1, 1)
     own_across(0, 0)
+    own_from_end(1, 1)
+    pass_across(0, 0)
+    prepare(1, 0)
     pass_to_end(0, 1, 1)
+    pass_to_end(0, 0, 1)
     pass_across(0, 1)
-    own_from_end(0, 0)
     loads["s", 0].wait()
     prepare(0, 0)
+    own_across(1, 1)
+    pass_to_end(0, 0, 2)
+    own_across(1, 0)
+    operand_from_end(1, 2, 0)
     prepare(0, 1)
-    loads["s", 1].wait()
-    prepare(1, 0)
-    prepare(1, 1)
-    pass_across(0, 0)
-    own_across(1, 0)
-    pass_to_end(0, 0, 1)
     pass_to_end(0, 1, 2)
-    own_from_end(1, 0)
-    pass_to_end(0, 0, 2)
-    own_from_end(1, 1)
+    operand_from_end(1, 0, 0)
+    own_to_end(1, 0)
+    operand_from_end(1, 1, 0)
     loads["wd", 0].wait()
     loads["wu", 0].wait()
     loads["g", 0].wait()
@@ -348,66 +411,63 @@
     pipe_send(2, True)
     pipe_send(2, False)
     pipe_wait(2)
+    pass_across(1, 1)
     backward(0, 1, ob.at[2])
     result(2).start()
-    grad_from_end(0, 0, 1)
-    grad_from_end(0, 1, 1)
-    grad_from_end(0, 1, 0)
-    pass_across(1, 1)
+    pass_to_end(1, 0, 1)
+    pass_across(1, 0)
+    pass_to_end(1, 0, 2)
+    pass_to_end(1, 1, 1)
     loads["x", 0].wait()
     forward(0, 0, yb.at[0])
-    pass_across(1, 0)
-    pass_to_end(1, 0, 1)
-    pass_to_end(1, 0, 2)
+    grad_from_end(0, 1, 0)
     own_to_end(1, 1)
+    grad_across(0, 1, 0)
+    grad_from_end(0, 0, 1)
+    grad_from_end(0, 0, 0)
+    grad_from_end(0, 1, 1)
+    pass_to_end(1, 1, 2)
     grad_across(0, 0, 1)
-    own_across(1, 1)
-    grad_from_end(0, 0, 0)
-    grad_across(0, 1, 0)
     grad_from_end(0, 2, 1)
-    grad_from_end(0, 2, 0)
-    pass_to_end(1, 1, 1)
-    pass_to_end(1, 1, 2)
-    grad_across(0, 1, 1)
-    own_to_end(1, 0)
-    grad_across(0, 0, 0)
     loads["wd", 1].wait()
     loads["wu", 1].wait()
     loads["g", 1].wait()
     end_gathers(1)
     backward(1, 0, bb.at[1])
-    pipe_send(3, True)
-    pipe_send(3, False)
     loads["x", 1].wait()
     forward(1, 0, yb.at[1])
+    pipe_send(1, True)
+    grad_across(0, 0, 0)
+    pipe_send(3, False)
+    pipe_send(3, True)
+    grad_across(0, 1, 1)
     pipe_send(0, True)
     pipe_wait(3)
     backward(1, 1, ob.at[3])
     result(3).start()
+    latents_from_end(1, 0)
+    pipe_send(1, False)
+    latents_arrive(1)
+    grad_from_end(1, 0, 1)
+    grad_to_end(0, 1)
+    grad_to_end(0, 0)
+    grad_across(1, 0, 0)
+    grad_from_end(1, 1, 1)
+    pipe_send(0, False)
     grad_across(1, 0, 1)
-    grad_to_end(0, 1)
+    grad_to_end(1, 0)
+    grad_across(1, 1, 0)
+    grad_from_end(0, 2, 0)
     grad_to_end(1, 1)
-    grad_across(1, 0, 0)
-    grad_from_end(1, 0, 1)
-    grad_to_end(0, 0)
-    grad_to_end(1, 0)
-    pipe_send(0, False)
-    grad_from_end(1, 0, 0)
-    grad_from_end(1, 1, 1)
-    grad_across(1, 1, 0)
-    pipe_send(1, False)
-    grad_from_end(1, 1, 0)
     grad_across(1, 1, 1)
-    pipe_send(1, True)
-    grad_from_end(1, 2, 0)
+    pipe_wait(1)
+    forward(1, 1, ob.at[1])
+    result(1).start()
     grad_from_end(1, 2, 1)
     grad_finish(0)
     pipe_wait(0)
     forward(0, 1, ob.at[0])
     result(0).start()
-    pipe_wait(1)
-    forward(1, 1, ob.at[1])
-    result(1).start()
     grad_finish(1)
 
     for m in range(2):
@@ -417,7 +477,13 @@
             def _(m=m, kind=kind):
                 ag_copy(m, kind, out_flow, 0, d, out_to, True).wait_send()
                 for j in range(3):
-                    rs_copy(m, out_flow, j, kind, out_to).wait_send()
+                    if kind in by_operands[m]:
+                        for which in ((0,), (1, 2))[kind]:
+                            operand(m, j, which).wait_send()
+                    else:
+                        rs_copy(m, out_flow, j, kind, out_to).wait_send()
+                if kind in by_operands[m]:
+                    latents_copy(m, kind).wait_send()
 
             @pl.when(is_mid)
             def _(m=m, kind=kind):
@@ -470,6 +536,10 @@
             vmem((2, 2, 3, latents, shard), BF16),
             vmem((2, shard, latents), BF16),
             vmem((2, latents, shard), BF16),
+            vmem((2, 3, shard, ticks * rows), BF16),
+            vmem((2, ticks * rows, latents), BF16),
+            vmem((2, 3, ticks * rows, shard), BF16),
+            vmem((2, latents, ticks * rows), BF16),
             dma((10,)),
             dma((8,)),
             dma((2, 2, 2, 3)),
@@ -478,6 +548,10 @@
             dma((4,)),
             dma((2, 2, 3, 2)),
             dma((2, 2, 3, 2)),
+            dma((2, 3, 3)),
+            dma((2, 3, 3)),
+            dma((2, 2)),
+            dma((2, 2)),
         ],
         compiler_params=pltpu.CompilerParams(
             collective_id=0, has_side_effects=True, vmem_limit_bytes=52 * 2**20

time: 242 us -> 228 us (0.942)
  Pallas kernels: 229 us -> 214 us
    pallas_call x1, Pallas kernels: 229 us -> 214 us  [body(): pl.pallas_call(kernel, out_shape=outs, in_specs=[pl.BlockSpec(memory_spac...]
where the time goes in v3:
time: 228 us; the launch traced here: 224 us
  Pallas kernels  214 us (94%)
  local copies, waits for them, and re-layouts  8.8 us (4%)
    pallas_call x1, Pallas kernels, body(): pl.pallas_call(kernel, out_shape=outs, in_specs=[pl.BlockSpec(memory_spac...  214 us
    unnamed x16, local copies, waits for them, and re-layouts  8.8 us

profile of v3, /device:TPU:6, one launch (start us, length us, event | category | flops | bytes accessed | tf_op | source)
XLA Modules:
  0.0 223.8 jit_solution(1420875171210262191)
XLA Ops:
  0.6 0.0 copy-start
  0.6 1.0 copy-done
  1.6 214.3 %relay_window.1 = (bf16[1,128,3072]{2,1,0:T(8,128)(2,1)}, bf16[1,128,3072]{2,1,0:T(8,128)(2,1)}, bf16[1,128,3072]{2,1,0:T(8,128)(2,1)}, bf16[1,128,3072]{2,1,0:T...) custom-call(bf16[1,128,3072]{2,1,0:T(8,128)(2,1)} %lf.1, ...), custom_call_target="tpu_custom_call" | custom-call | tf_op jit(solution)/shard_map/relay_window/pallas_call | solution.py:517
  216.0 0.0 copy-start.3
  216.0 0.0 copy-start.2
  216.0 2.2 copy.26
  218.2 0.0 copy-done.3
  218.2 0.0 copy-start.1
  218.2 0.9 copy.27
  219.1 0.0 copy-done.2
  219.1 0.9 copy.28
  219.9 0.0 copy-done.1
  219.9 0.9 copy.29
  220.8 0.7 copy.30
  221.6 0.7 copy.31
  222.3 0.7 copy.32
  223.1 0.7 copy.33
Async XLA Ops:
  0.6 1.0 copy-start
  216.0 2.2 copy-start.3
  216.0 3.1 %copy-start.2 = (bf16[1,128,3072]{2,1,0:T(8,128)(2,1)S(1)}, bf16[1,128,3072]{2,1,0:T(8,128)(2,1)}, u32[]{:S(2)}) copy-start(bf16[1,128,3072]{2,1,0:T(8,128)(2,1)} %get-tuple-element.18) | copy-start | bytes 2359300
  218.2 1.8 copy-start.1

commit v4 on v3

--- a/solution.py
+++ b/solution.py
@@ -504,6 +504,11 @@
         result(n).wait()
 
 
+def hand_over(*refs):
+    for source, target in zip(refs[:8], refs[8:]):
+        target[...] = source[...]
+
+
 def body(*arrays):
     lf, ls, ld, lu = arrays[0], arrays[4], arrays[6], arrays[7]
     _, ticks, rows, width = ls.shape
@@ -514,7 +519,7 @@
     ] * 2
     vmem = pltpu.VMEM
     dma = pltpu.SemaphoreType.DMA
-    return pl.pallas_call(
+    results = pl.pallas_call(
         kernel,
         out_shape=outs,
         in_specs=[pl.BlockSpec(memory_space=pl.ANY)] * 10,
@@ -554,10 +559,22 @@
             dma((2, 2)),
         ],
         compiler_params=pltpu.CompilerParams(
-            collective_id=0, has_side_effects=True, vmem_limit_bytes=52 * 2**20
+            collective_id=0, has_side_effects=True, vmem_limit_bytes=62 * 2**20
         ),
         name="relay_window",
     )(*arrays)
+    parts = 2
+    blocks = [
+        pl.BlockSpec((1, out.shape[1] // parts, out.shape[2]), lambda n: (0, n, 0)) for out in outs
+    ]
+    return pl.pallas_call(
+        hand_over,
+        grid=(parts,),
+        out_shape=outs,
+        in_specs=blocks,
+        out_specs=blocks,
+        name="hand_over",
+    )(*results)
 
 
 def solution(mesh):

time: 228 us -> 224 us (0.982)
  local copies, waits for them, and re-layouts: 8.8 us -> 0 us
  Pallas kernels: 214 us -> 219 us
    unnamed x16 -> x0, local copies, waits for them, and re-layouts: 8.8 us -> none
    pallas_call x0 -> x1, Pallas kernels: none -> 3.93 us  [body(): pl.pallas_call(hand_over, grid=(parts,), out_shape=outs, in_specs=blocks,...]
where the time goes in v4:
time: 224 us; the launch traced here: 220 us
  Pallas kernels  219 us (98%)
    pallas_call x1, Pallas kernels, body(): pl.pallas_call(kernel, out_shape=outs, in_specs=[pl.BlockSpec(memory_spac...  215 us

profile of v4, /device:TPU:6, one launch (start us, length us, event | category | flops | bytes accessed | tf_op | source)
XLA Modules:
  0.0 219.5 jit_solution(17537923285083166678)
XLA Ops:
  0.6 215.0 %relay_window.1 = (bf16[1,128,3072]{2,1,0:T(8,128)(2,1)}, bf16[1,128,3072]{2,1,0:T(8,128)(2,1)}, bf16[1,128,3072]{2,1,0:T(8,128)(2,1)}, bf16[1,128,3072]{2,1,0:T...) custom-call(bf16[1,128,3072]{2,1,0:T(8,128)(2,1)} %lf.1, ...), custom_call_target="tpu_custom_call" | custom-call | tf_op jit(solution)/shard_map/relay_window/pallas_call | solution.py:522
  215.6 3.9 %hand_over.1 = (bf16[1,128,3072]{2,1,0:T(8,128)(2,1)}, bf16[1,128,3072]{2,1,0:T(8,128)(2,1)}, bf16[1,128,3072]{2,1,0:T(8,128)(2,1)}, bf16[1,128,3072]{2,1,0:T(8,...) custom-call(bf16[1,128,3072]{2,1,0:T(8,128)(2,1)} %get-tuple-element, ...), custom_call_target="tpu_custom_call" | custom-call | tf_op jit(solution)/shard_map/hand_over/pallas_call | solution.py:570
